TPU v7x, 32 devices: a whole 2x2x4 slice. The times are simulated.
32 devices in a mesh: dp: 8 (over z, core), tensor: 4 (over y, x).
Axes of the slice: x: 2, y: 2, z: 4, core: 2. Of those that a mesh axis runs over, the one named last changes fastest.
Arguments:
- inputs: bfloat16 [2048, 2560], P('dp'), may hold values from -6 to 6
- old_weight: bfloat16 [2560, 2048], P('dp', 'tensor'), may hold values from -0.125 to 0.125
- keep_cols: int32 [1536], replicated, may hold values from 0 to 2047, as said below
- owner: int32 [12], replicated, may hold values from 0 to 3, as said below
- out_grad: bfloat16 [2048, 1536], P('dp', 'tensor'), may hold values from -6 to 6
Outputs:
- projected: bfloat16 [2048, 1536], P('dp', 'tensor')
- gradient_input: bfloat16 [2048, 2560], P('dp', 'tensor')
- weight_grad: float32 [2560, 1536], P('dp', 'tensor')
Inputs may be any that keep to these rules, and one draw needn't show every extreme that they name: Each index t of tensor holds old columns [t * 4 * 128, (t + 1) * 4 * 128) and keeps exactly 384 of them, so blocks t * 3 to t * 3 + 2 of keep_cols come from holder t. Every owner receives exactly 3 blocks, and at most 2 blocks from one old holder; some owner receives 2 from one holder.
All inputs are finite; a program needn't handle non-finite values.
Results may differ from a plain program's by a relative error of at most 0.015.
Values may be sent and summed in bfloat16 or wider, within the bound.
A program may use at most 64 MiB of HBM per device.

v0:
```python
import jax
import jax.numpy as jnp
from jax import lax
from jax.sharding import PartitionSpec as P


def local(inputs, old_weight, keep_cols, owner, out_grad):
    groups = lax.axis_size("tensor")
    myself = lax.axis_index("tensor")
    blocks = owner.shape[0]
    own_blocks = blocks // groups
    keep_table = keep_cols.reshape(blocks, 128)
    block_ids = jnp.arange(blocks, dtype=jnp.int32)
    earlier = block_ids[None, :] < block_ids[:, None]
    same_owner = owner[:, None] == owner[None, :]
    owner_rank = jnp.sum(same_owner & earlier, axis=1)
    ranks_here = jnp.arange(own_blocks, dtype=jnp.int32)
    mine_match = (owner[None, :] == myself) & (owner_rank[None, :] == ranks_here[:, None])
    mine_ids = jnp.sum(jnp.where(mine_match, block_ids[None, :], 0), axis=1)
    every_column = lax.all_gather(old_weight, "tensor", axis=1, tiled=True)
    new_stripe = jnp.take(every_column, keep_table[mine_ids].reshape(-1), axis=1)
    expanded_output = inputs.astype(jnp.float32)
    inverse_sigma = lax.rsqrt(
        jnp.mean(expanded_output * expanded_output, axis=1, keepdims=True) + 1e-05
    )
    centered_input = expanded_output * inverse_sigma
    normalized_rows = centered_input.astype(jnp.bfloat16)
    tokens, width = inputs.shape
    piece = lax.all_gather(new_stripe, "dp", axis=0, tiled=True)
    normed_cols = normalized_rows
    proj_sum = jnp.dot(normed_cols, piece, preferred_element_type=jnp.float32)
    partial_term = lax.dot_general(
        out_grad, piece, (((1,), (1,)), ((), ())), preferred_element_type=jnp.float32
    )
    back_sum = partial_term
    proj_sum, back_sum = (proj_sum, back_sum)
    projected = proj_sum.astype(jnp.bfloat16)
    share = width // groups
    reduced_total = lax.psum(back_sum.astype(jnp.bfloat16), "tensor").astype(jnp.float32)
    inner_product = jnp.mean(reduced_total * centered_input, axis=1, keepdims=True)
    complete_gradient = inverse_sigma * (reduced_total - centered_input * inner_product)
    gradient_input = lax.dynamic_slice_in_dim(complete_gradient, myself * share, share, 1).astype(
        jnp.bfloat16
    )
    normed_cols = normalized_rows
    weight_grad = lax.psum_scatter(
        lax.dot_general(
            normed_cols, out_grad, (((0,), (0,)), ((), ())), preferred_element_type=jnp.float32
        ),
        "dp",
        scatter_dimension=0,
        tiled=True,
    )
    return (projected, gradient_input, weight_grad)


def solution(mesh):
    placed = (P("dp", None), P("dp", "tensor"), P(), P(), P("dp", "tensor"))
    return jax.shard_map(
        local,
        mesh=mesh,
        in_specs=placed,
        out_specs=(P("dp", "tensor"), P("dp", "tensor"), P("dp", "tensor")),
        check_vma=False,
    )
```

profile of v0, /device:TPU:6, one launch (start us, length us, event | category | flops | bytes accessed | tf_op | source)
XLA Modules:
  0.0 192.0 jit_solution(2342627788450787116)
XLA Ops:
  7.2 0.0 copy-start
  7.2 0.0 all-gather.3.cloned.1.call-start
  7.2 1.9 %copy.16 = bf16[320,512]{0,1:T(8,128)(2,1)} copy(bf16[320,512]{1,0:T(8,128)(2,1)} %param.6) | data formatting | bytes 655360 | tf_op args[1]
  9.2 0.0 all-gather.3.cloned.1.call-update
  9.2 0.0 all-gather.5.cloned.1.call-start
  9.2 0.9 convert_reduce_fusion
  10.1 0.7 broadcast_compare_fusion
  10.8 0.1 select_reduce_fusion
  10.9 1.3 gather_fusion
  12.3 29.5 %all-gather.3.cloned.1.call-done = bf16[320,2048]{0,1:T(8,128)(2,1)} async-done(((bf16[320,512]{0,1:T(8,128)(2,1)}), bf16[320,2048]{0,1:T(8,128)(2,1)}) %all-gather.3.cloned.1.call-update) | async-done | bytes 1310736 | tf_op jit(solution)/shard_map/all_gather | solution.py:20
  41.7 3.6 %gather_fusion.1 = bf16[384,320]{1,0:T(8,128)(2,1)S(1)} fusion(bf16[320,2048]{0,1:T(8,128)(2,1)} %all-gather.3.cloned.1.call-done, s32[1024]{0:T(1024)S(1)} %pad_clamp_fusion), kind=kCustom, calls=%fused_computation.1 | custom fusion | bytes 493056 | tf_op jit(solution)/shard_map/jit(_take)/gather | solution.py:21
  45.3 0.1 select_bitcast_fusion
  45.5 0.9 copy.17
  46.3 0.0 all-gather.5.cloned.1.call-update
  46.3 0.0 copy-start.3
  46.4 0.0 all-reduce.2.cloned.1.call-start
  46.4 29.0 %all-gather.5.cloned.1.call-done = bf16[2560,384]{1,0:T(8,128)(2,1)} async-done(((bf16[320,384]{1,0:T(8,128)(2,1)}), bf16[2560,384]{1,0:T(8,128)(2,1)}) %all-gather.5.cloned.1.call-update) | async-done | bytes 1966096 | tf_op jit(solution)/shard_map/all_gather | solution.py:29
  75.4 0.0 copy-done
  75.4 3.5 %fusion = bf16[256,2560]{0,1:T(8,128)(2,1)} fusion(bf16[2560,384]{1,0:T(8,128)(2,1)} %all-gather.5.cloned.1.call-done, bf16[256,384]{1,0:T(8,128)(2,1)S(1)} %copy-done), kind=kOutput, calls=%fused_computation.3 | convolution fusion | flops 503971840 | bytes 3473408 | tf_op jit(solution)/shard_map/dot_general | solution.py:32
  78.9 0.0 all-reduce.2.cloned.1.call-update
  79.0 0.0 reduce-scatter.2.cloned.1.call-start
  79.0 0.0 copy-done.3
  79.0 0.6 copy.15
  79.6 0.4 fusion.1
  80.0 2.7 %fusion.3 = f32[2560,384]{1,0:T(8,128)} fusion(bf16[256,384]{1,0:T(8,128)(2,1)S(1)} %copy-done, f32[256]{0:T(256)S(1)} %add_rsqrt_fusion, bf16[256,2560]{0,1:T(8,128)(2,1)S(1)} %copy.15), kind=kOutput, calls=%fused_computation.10 | convolution fusion | flops 505282560 | bytes 5440512 | tf_op jit(solution)/shard_map/dot_general | solution.py:47
  82.8 0.0 copy-start.2
  82.8 0.0 reduce-scatter.2.cloned.1.call-update
  82.8 1.5 copy-done.2
  84.3 1.6 convolution_convert_fusion.1
  85.9 48.3 %all-reduce.2.cloned.1.call-done = bf16[256,2560]{0,1:T(8,128)(2,1)} async-done(((bf16[256,2560]{0,1:T(8,128)(2,1)}), bf16[256,2560]{0,1:T(8,128)(2,1)}) %all-reduce.2.cloned.1.call-update) | async-done | bytes 1310736 | tf_op jit(solution)/shard_map/psum | solution.py:39
  134.2 0.0 copy-start.1
  134.2 1.6 convert_element_type.30
  135.8 0.1 copy-done.1
  135.9 0.6 multiply_reduce_fusion
  136.5 0.1 fusion.7
  136.6 0.9 copy.18
  137.5 47.9 %reduce-scatter.2.cloned.1.call-done = f32[320,384]{1,0:T(8,128)} async-done(((f32[2560,384]{1,0:T(8,128)}), f32[320,384]{1,0:T(8,128)}) %reduce-scatter.2.cloned.1.call-update) | async-done | bytes 491536 | tf_op jit(solution)/shard_map/reduce_scatter | solution.py:46
  (7 shorter events, 0.1 us)
Async XLA Ops:
  7.2 68.3 %copy-start = (bf16[256,384]{1,0:T(8,128)(2,1)S(1)}, bf16[256,384]{1,0:T(8,128)(2,1)}, u32[]{:S(2)}) copy-start(bf16[256,384]{1,0:T(8,128)(2,1)} %param.9) | copy-start | bytes 589828
  7.2 34.5 %all-gather.3.cloned.1.call-start = ((), (), s32[]{:S(2)}) async-start(), calls=%async_computation.1 | async-start | bytes 1966080 | tf_op jit(solution)/shard_map/all_gather | solution.py:20
  9.2 66.2 %all-gather.5.cloned.1.call-start = ((), (), s32[]{:S(2)}) async-start(), calls=%async_computation.2 | async-start | bytes 2211840 | tf_op jit(solution)/shard_map/all_gather | solution.py:29
  46.3 32.7 %copy-start.3 = (bf16[256,2560]{1,0:T(8,128)(2,1)S(1)}, bf16[256,2560]{1,0:T(8,128)(2,1)}, u32[]{:S(2)}) copy-start(bf16[256,2560]{1,0:T(8,128)(2,1)} %param.5) | copy-start | bytes 3932164
  46.4 87.8 %all-reduce.2.cloned.1.call-start = ((), (), s32[]{:S(2)}) async-start(), calls=%async_computation.3 | async-start | bytes 2621440 | tf_op jit(solution)/shard_map/psum | solution.py:39
  79.0 106.5 %reduce-scatter.2.cloned.1.call-start = ((), (), s32[]{:S(2)}) async-start(), calls=%async_computation.4 | async-start | bytes 4423680 | tf_op jit(solution)/shard_map/reduce_scatter | solution.py:46
  82.8 1.6 copy-start.2
  134.2 1.7 copy-start.1
Sparse Core Ops, SparseCore 0:
  10.4 31.2 all-gather.2
  46.5 28.9 all-gather.4
  79.1 55.0 all-reduce.1
  136.9 48.4 reduce-scatter.1
where the time goes:
time: 194 us; the launch traced here: 192 us
  waiting for transfers between devices  155 us (80%)
  between operations  13.8 us (7%)
  local copies, waits for them, and re-layouts  10.8 us (6%)
  matrix products  7.8 us (4%)
  other arithmetic  4.54 us (2%)
    psum x1, waiting for transfers between devices, local(): lax.psum(back_sum.astype(jnp.bfloat16), 'tensor').astype(jnp.float32)  48.3 us
    reduce_scatter x1, waiting for transfers between devices, local(): lax.psum_scatter(lax.dot_general(normed_cols, out_grad, (((0,), (0,)), ((...  47.9 us
    all_gather x1, waiting for transfers between devices, local(): every_column = lax.all_gather(old_weight, 'tensor', axis=1, tiled=True)  29.5 us
    all_gather x1, waiting for transfers between devices, local(): piece = lax.all_gather(new_stripe, 'dp', axis=0, tiled=True)  29 us
    unnamed x11, local copies, waits for them, and re-layouts  5.07 us
  transfers between devices with their start and end apart: 4, of which 4 were waited for; matrix products, arithmetic and copies ran while one was open for 6% of the time, Pallas kernels for 0%

commit v1 on v0

--- a/solution.py
+++ b/solution.py
@@ -1,10 +1,383 @@
+import functools
+
 import jax
 import jax.numpy as jnp
 from jax import lax
+from jax.experimental import pallas as pl
+from jax.experimental.pallas import tpu as pltpu
 from jax.sharding import PartitionSpec as P
 
-
-def local(inputs, old_weight, keep_cols, owner, out_grad):
+MESH = pl.DeviceIdType.MESH
+BF16 = jnp.bfloat16
+F32 = jnp.float32
+
+
+def fused_kernel(
+    groups, ranks, x_ref, old_ref, keep_ref, owner_ref, og_ref,
+    proj_ref, gin_ref, wg_ref,
+    comp, pack, unpacked, xhat, normed, stripes, acc, dn_send, dn_recv, dot_send, dot_recv,
+    sib_send, sib_recv, up_send, up_recv, down_send, down_recv,
+    pack_ss, pack_rs, sib_ss, sib_rs, up_ss, up_rs, down_ss, down_rs,
+    gup_ss, gdown_ss, gsib_ss, gather_rs, dn_ss, dn_rs, dot_ss, dot_rs,
+):
+    dp = lax.axis_index("dp")
+    ten = lax.axis_index("tensor")
+    chips = ranks // 2
+    z, core = dp // 2, dp % 2
+    rows, width = old_ref.shape
+    tokens, features = x_ref.shape
+    blocks = owner_ref.shape[0]
+    own = blocks // groups
+    per = ranks // groups
+    share = features // groups
+    sibling = z * 2 + (1 - core)
+
+    def peer(k):
+        return lax.rem(ten + k, groups)
+
+    def remote(src, dst, ss, rs, **where):
+        return pltpu.make_async_remote_copy(
+            src_ref=src, dst_ref=dst, send_sem=ss, recv_sem=rs,
+            device_id=where, device_id_type=MESH,
+        )
+
+    barrier = pltpu.get_barrier_semaphore()
+    for k in range(1, groups):
+        pl.semaphore_signal(barrier, inc=1, device_id={"tensor": peer(k)}, device_id_type=MESH)
+    pl.semaphore_signal(barrier, inc=1, device_id={"dp": sibling}, device_id_type=MESH)
+
+    @pl.when(z > 0)
+    def _():
+        pl.semaphore_signal(barrier, inc=1, device_id={"dp": dp - 2}, device_id_type=MESH)
+
+    @pl.when(z < chips - 1)
+    def _():
+        pl.semaphore_signal(barrier, inc=1, device_id={"dp": dp + 2}, device_id_type=MESH)
+
+    column = lax.broadcasted_iota(jnp.int32, (width, 128), 0) + ten * width
+    for i in range(own):
+        pick = jnp.where(column == keep_ref[pl.ds(ten * own + i, 1), :], 1.0, 0.0).astype(BF16)
+        comp[i] = jnp.dot(old_ref[...], pick, preferred_element_type=F32).astype(BF16)
+    for k in range(groups):
+        target = peer(k)
+        first = jnp.int32(own - 1)
+        for i in range(own - 2, -1, -1):
+            first = jnp.where(owner_ref[ten * own + i] == target, i, first)
+        second = jnp.int32(own - 1)
+        for i in range(own - 2, 0, -1):
+            hit = (owner_ref[ten * own + i] == target) & (i > first)
+            second = jnp.where(hit, i, second)
+        dst = unpacked if k == 0 else pack
+        dst[k, 0] = comp[first]
+        dst[k, 1] = comp[second]
+
+    ends = jnp.where(z > 0, 1, 0) + jnp.where(z < chips - 1, 1, 0)
+    pl.semaphore_wait(barrier, groups + ends)
+
+    def pack_copy(k):
+        return remote(pack.at[k], unpacked.at[k], pack_ss.at[k], pack_rs.at[k], tensor=peer(k))
+
+    for k in range(1, groups):
+        pack_copy(k).start()
+
+    total = jnp.zeros((1, tokens), F32)
+    for j in range(features // 128):
+        part = x_ref[:, j * 128:(j + 1) * 128].astype(F32).T
+        xhat[j * 128:(j + 1) * 128, :] = part
+        total = total + jnp.sum(part * part, axis=0, keepdims=True)
+    inv = lax.rsqrt(total / features + 1e-05)
+    for j in range(features // 128):
+        part = xhat[j * 128:(j + 1) * 128, :] * inv
+        xhat[j * 128:(j + 1) * 128, :] = part
+        normed[j * 128:(j + 1) * 128, :] = part.astype(BF16)
+
+    def strip(ref, d):
+        return ref[pl.ds(pl.multiple_of(d * rows, 16), rows), :]
+
+    def grad_part(d):
+        return jnp.dot(strip(normed, d), og_ref[...], preferred_element_type=F32)
+
+    def sib_copy(c):
+        return remote(sib_send.at[c], sib_recv.at[c], sib_ss.at[c], sib_rs.at[c], dp=sibling)
+
+    def up_copy(c):
+        return remote(up_send.at[c], up_recv.at[c], up_ss.at[c], up_rs.at[c], dp=dp + 2)
+
+    def down_copy(c):
+        return remote(down_send.at[c], down_recv.at[c], down_ss.at[c], down_rs.at[c], dp=dp - 2)
+
+    order = []
+    for k in range(chips):
+        for c in (chips - 1 - k, k):
+            if c not in order:
+                order.append(c)
+    for c in order:
+        sib_send[c] = grad_part(2 * c + 1 - core).astype(BF16)
+        sib_copy(c).start()
+
+    def pair_sum(c):
+        mine = grad_part(2 * c + core)
+        sib_copy(c).wait_recv()
+        return mine + sib_recv[c].astype(F32)
+
+    def up_first(c):
+        up_send[c] = pair_sum(c).astype(BF16)
+        up_copy(c).start()
+
+    def down_first(c):
+        down_send[c] = pair_sum(c).astype(BF16)
+        down_copy(c).start()
+
+    @pl.when(z == 0)
+    def _():
+        for c in range(chips - 1, 0, -1):
+            up_first(c)
+
+    @pl.when(z == chips - 1)
+    def _():
+        for c in range(chips - 1):
+            down_first(c)
+
+    def chain(k):
+        up, down = chips - 1 - k, k
+
+        @pl.when((z > 0) & (z < up))
+        def _():
+            mine = pair_sum(up)
+            up_copy(up).wait_recv()
+            up_send[up] = (mine + up_recv[up].astype(F32)).astype(BF16)
+            up_copy(up).start()
+
+        @pl.when((z < chips - 1) & (z > down))
+        def _():
+            mine = pair_sum(down)
+            down_copy(down).wait_recv()
+            down_send[down] = (mine + down_recv[down].astype(F32)).astype(BF16)
+            down_copy(down).start()
+
+    places = [jnp.int32(0) for _ in range(own)]
+    count = jnp.int32(0)
+    for h in range(groups):
+        slot = jnp.int32(0)
+        k = lax.rem(ten - h + groups, groups)
+        for i in range(own):
+            hit = owner_ref[h * own + i] == ten
+            for r in range(own):
+                places[r] = jnp.where(hit & (count == r), k * 2 + slot, places[r])
+            step = jnp.where(hit, 1, 0)
+            slot, count = slot + step, count + step
+    for k in range(1, groups):
+        pack_copy(k).wait_recv()
+    for r in range(own):
+        stripes[dp, :, r * 128:(r + 1) * 128] = unpacked[places[r] // 2, places[r] % 2]
+
+    def gather_up(d):
+        return remote(stripes.at[d], stripes.at[d], gup_ss.at[d], gather_rs.at[d], dp=dp + 2)
+
+    def gather_down(d):
+        return remote(stripes.at[d], stripes.at[d], gdown_ss.at[d], gather_rs.at[d], dp=dp - 2)
+
+    def gather_sib(d):
+        return remote(stripes.at[d], stripes.at[d], gsib_ss.at[d], gather_rs.at[d], dp=sibling)
+
+    def dn_copy(d):
+        k = lax.rem(d // per - ten + groups, groups)
+        j = d % per
+        return remote(
+            dn_send.at[d], dn_recv.at[k, j], dn_ss.at[d], dn_rs.at[k, j], tensor=d // per
+        )
+
+    def use(d):
+        part = lax.dot_general(
+            stripes[d], og_ref[...], (((1,), (1,)), ((), ())), preferred_element_type=F32
+        ).astype(BF16)
+        dn_send[d] = part
+
+        @pl.when(d // per != ten)
+        def _():
+            dn_copy(d).start()
+
+        dot_send[...] += jnp.sum(
+            (part.astype(F32) * strip(xhat, d)).reshape(rows // 8, 8, tokens), axis=0
+        )
+        acc[...] += lax.dot_general(
+            strip(normed, d), stripes[d], (((0,), (0,)), ((), ())), preferred_element_type=F32
+        )
+
+    acc[...] = jnp.zeros_like(acc)
+    dot_send[...] = jnp.zeros_like(dot_send)
+
+    @pl.when(z < chips - 1)
+    def _():
+        gather_up(dp).start()
+
+    @pl.when(z > 0)
+    def _():
+        gather_down(dp).start()
+
+    gather_sib(dp).start()
+    use(dp)
+
+    def from_sibling(chip):
+        d = chip * 2 + 1 - core
+        gather_sib(d).wait_recv()
+        use(d)
+
+    for s in range(1, chips):
+        chain(s - 1)
+
+        @pl.when(z - s >= 0)
+        def _():
+            d = dp - 2 * s
+            gather_up(d).wait_recv()
+
+            @pl.when(z < chips - 1)
+            def _():
+                gather_up(d).start()
+
+            gather_sib(d).start()
+
+        @pl.when(z + s < chips)
+        def _():
+            d = dp + 2 * s
+            gather_down(d).wait_recv()
+
+            @pl.when(z > 0)
+            def _():
+                gather_down(d).start()
+
+            gather_sib(d).start()
+
+        if s == 1:
+            from_sibling(z)
+
+        @pl.when(z - s >= 0)
+        def _():
+            use(dp - 2 * s)
+            from_sibling(z - s)
+
+        @pl.when(z + s < chips)
+        def _():
+            use(dp + 2 * s)
+            from_sibling(z + s)
+
+    def dot_copy(k):
+        return remote(dot_send, dot_recv.at[k], dot_ss.at[k], dot_rs.at[k], tensor=peer(k))
+
+    for k in range(1, groups):
+        dot_copy(k).start()
+    proj_ref[...] = acc[...].astype(BF16)
+
+    sib_total = grad_part(dp)
+    sib_copy(z).wait_recv()
+    wg_ref[...] = sib_total + sib_recv[z].astype(F32)
+
+    @pl.when(z > 0)
+    def _():
+        up_copy(z).wait_recv()
+        wg_ref[...] += up_recv[z].astype(F32)
+
+    @pl.when(z < chips - 1)
+    def _():
+        down_copy(z).wait_recv()
+        wg_ref[...] += down_recv[z].astype(F32)
+
+    dot = dot_send[...]
+    for k in range(1, groups):
+        dot_copy(k).wait_recv()
+        dot = dot + dot_recv[k]
+    mean = jnp.sum(dot, axis=0, keepdims=True) / features
+    for j in range(per):
+        at = ten * per + j
+        full = dn_send[at].astype(F32)
+        for k in range(1, groups):
+            remote(
+                dn_send.at[at], dn_recv.at[k, j], dn_ss.at[at], dn_rs.at[k, j], tensor=peer(k)
+            ).wait_recv()
+            full = full + dn_recv[k, j].astype(F32)
+        acc_t = inv * (full - strip(xhat, at) * mean)
+        xhat[pl.ds(pl.multiple_of(at * rows, 16), rows), :] = acc_t
+    for j in range(share // 128):
+        rows_j = pl.ds(pl.multiple_of(ten * share + j * 128, 128), 128)
+        gin_ref[:, j * 128:(j + 1) * 128] = xhat[rows_j, :].T.astype(BF16)
+
+    for k in range(1, groups):
+        pack_copy(k).wait_send()
+        dot_copy(k).wait_send()
+    for c in range(chips):
+        sib_copy(c).wait_send()
+
+        @pl.when(c > z)
+        def _():
+            up_copy(c).wait_send()
+
+        @pl.when(c < z)
+        def _():
+            down_copy(c).wait_send()
+
+        d = 2 * c + core
+        gather_sib(d).wait_send()
+
+        @pl.when((c <= z) & (z < chips - 1))
+        def _():
+            gather_up(d).wait_send()
+
+        @pl.when((c >= z) & (z > 0))
+        def _():
+            gather_down(d).wait_send()
+
+    for d in range(ranks):
+        @pl.when(d // per != ten)
+        def _():
+            dn_copy(d).wait_send()
+
+
+def fused(groups, ranks, inputs, old_weight, keep_cols, owner, out_grad):
+    tokens, features = inputs.shape
+    rows, _ = old_weight.shape
+    cols = out_grad.shape[1]
+    own = cols // 128
+    chips = ranks // 2
+    per = ranks // groups
+    stripe = (rows, cols)
+    dma = pltpu.SemaphoreType.DMA
+    vmem = pl.BlockSpec(memory_space=pltpu.VMEM)
+    smem = pl.BlockSpec(memory_space=pltpu.SMEM)
+    return pl.pallas_call(
+        functools.partial(fused_kernel, groups, ranks),
+        out_shape=(
+            jax.ShapeDtypeStruct((tokens, cols), BF16),
+            jax.ShapeDtypeStruct((tokens, features // groups), BF16),
+            jax.ShapeDtypeStruct(stripe, F32),
+        ),
+        in_specs=[vmem, vmem, vmem, smem, vmem],
+        out_specs=(vmem, vmem, vmem),
+        scratch_shapes=[
+            pltpu.VMEM((own, rows, 128), BF16),
+            pltpu.VMEM((groups, 2, rows, 128), BF16),
+            pltpu.VMEM((groups, 2, rows, 128), BF16),
+            pltpu.VMEM((features, tokens), F32),
+            pltpu.VMEM((features, tokens), BF16),
+            pltpu.VMEM((ranks,) + stripe, BF16),
+            pltpu.VMEM((tokens, cols), F32),
+            pltpu.VMEM((ranks, rows, tokens), BF16),
+            pltpu.VMEM((groups, per, rows, tokens), BF16),
+            pltpu.VMEM((8, tokens), F32),
+            pltpu.VMEM((groups, 8, tokens), F32),
+        ]
+        + [pltpu.VMEM((chips,) + stripe, BF16)] * 6
+        + [dma((groups,))] * 2
+        + [dma((chips,))] * 6
+        + [dma((ranks,))] * 5
+        + [dma((groups, per))]
+        + [dma((groups,))] * 2,
+        compiler_params=pltpu.CompilerParams(
+            collective_id=0, has_side_effects=True, vmem_limit_bytes=56 * 1024 * 1024
+        ),
+    )(inputs, old_weight, keep_cols.reshape(-1, 128), owner, out_grad)
+
+
+def plain(inputs, old_weight, keep_cols, owner, out_grad):
     groups = lax.axis_size("tensor")
     myself = lax.axis_index("tensor")
     blocks = owner.shape[0]
@@ -55,7 +428,16 @@
 
 
 def solution(mesh):
+    groups, ranks = mesh.shape["tensor"], mesh.shape["dp"]
     placed = (P("dp", None), P("dp", "tensor"), P(), P(), P("dp", "tensor"))
+
+    def local(inputs, old_weight, keep_cols, owner, out_grad):
+        rows, share = old_weight.shape[0], inputs.shape[1] // groups
+        fits = rows % 16 == 0 and share % 128 == 0 and ranks % groups == 0 and ranks % 2 == 0
+        if fits:
+            return fused(groups, ranks, inputs, old_weight, keep_cols, owner, out_grad)
+        return plain(inputs, old_weight, keep_cols, owner, out_grad)
+
     return jax.shard_map(
         local,
         mesh=mesh,

time: 194 us -> 68 us (0.35)
  waiting for transfers between devices: 155 us -> 0 us
  Pallas kernels: 0 us -> 62.8 us
  between operations: 13.8 us -> 0.65 us
  matrix products: 7.8 us -> 0 us
  local copies, waits for them, and re-layouts: 10.8 us -> 4.18 us
  other arithmetic: 4.54 us -> 0 us
    pallas_call x0 -> x1, Pallas kernels: none -> 62.8 us  [fused(): pl.pallas_call(functools.partial(fused_kernel, groups, ranks), out_shape=...]
    all_gather x2 -> x0, waiting for transfers between devices: 58.5 us -> none  [the longest x1 29.5 us: local(): every_column = lax.all_gather(old_weight, 'tensor', axis=1, tiled=True)]
    psum x1 -> x0, waiting for transfers between devices: 48.3 us -> none  [local(): lax.psum(back_sum.astype(jnp.bfloat16), 'tensor').astype(jnp.float32)]
    reduce_scatter x1 -> x0, waiting for transfers between devices: 47.9 us -> none  [local(): lax.psum_scatter(lax.dot_general(normed_cols, out_grad, (((0,), (0,)), ((...]
    dot_general x3 -> x0, matrix products: 7.8 us -> none  [the longest x1 3.51 us: local(): lax.dot_general(out_grad, piece, (((1,), (1,)), ((), ())), preferred_elem...]
    gather x2 -> x0, local copies, waits for them, and re-layouts: 4.87 us -> none  [the longest x1 3.61 us: local(): jnp.take(every_column, keep_table[mine_ids].reshape(-1), axis=1)]
    reduce_sum x4 -> x0, other arithmetic: 1.96 us -> none  [the longest x1 0.91 us: local(): owner_rank = jnp.sum(same_owner & earlier, axis=1)]
    unnamed x11 -> x5, local copies, waits for them, and re-layouts: 5.07 us -> 4.18 us
  transfers between devices with their start and end apart: 4 -> 0, of which waited for: 4 -> 0; matrix products, arithmetic and copies ran while one was open for 6% -> 0% of each run, Pallas kernels for 0% -> 0%
where the time goes in v1:
time: 68 us; the launch traced here: 67.6 us
  Pallas kernels  62.8 us (92%)
  local copies, waits for them, and re-layouts  4.18 us (6%)
    pallas_call x1, Pallas kernels, fused(): pl.pallas_call(functools.partial(fused_kernel, groups, ranks), out_shape=...  62.8 us
    unnamed x5, local copies, waits for them, and re-layouts  4.18 us

profile of v1, /device:TPU:6, one launch (start us, length us, event | category | flops | bytes accessed | tf_op | source)
XLA Modules:
  0.0 67.6 jit_solution(16199497749715140866)
XLA Ops:
  0.6 62.8 %shard_map.76 = (bf16[256,384]{1,0:T(8,128)(2,1)}, bf16[256,640]{1,0:T(8,128)(2,1)}, f32[320,384]{1,0:T(8,128)}) custom-call(bf16[256,2560]{1,0:T(8,128)(2,1)} %x_ref.1, bf16[320,512]{1,0:T(8,128)(2,1)} %old_ref.1, s32[12,128]{1,0:T(8,128)} %bitcast.1, s32[12]{0:T(128)} %owner_ref.1, bf16[256,384]{1,0:T(8,128)(2,1)} %og_ref.1), custom_call_target="tpu_custom_call" | custom-call | tf_op jit(solution)/shard_map/pallas_call | solution.py:346
  63.4 0.0 copy-start
  63.4 1.7 %copy.11 = bf16[256,384]{1,0:T(8,128)(2,1)} copy(bf16[256,384]{1,0:T(8,128)(2,1)} %get-tuple-element.6) | data formatting | bytes 393216
  65.1 1.7 %copy.12 = bf16[256,640]{1,0:T(8,128)(2,1)} copy(bf16[256,640]{1,0:T(8,128)(2,1)} %get-tuple-element.7) | data formatting | bytes 655360
  66.8 0.0 copy-done
  66.8 0.8 %copy.13 = f32[320,384]{1,0:T(8,128)} copy(f32[320,384]{1,0:T(8,128)S(1)} %copy-done) | data formatting | bytes 983040
Async XLA Ops:
  63.4 3.4 %copy-start = (f32[320,384]{1,0:T(8,128)S(1)}, f32[320,384]{1,0:T(8,128)}, u32[]{:S(2)}) copy-start(f32[320,384]{1,0:T(8,128)} %get-tuple-element.8) | copy-start | bytes 1474564

commit v2 on v1

--- a/solution.py
+++ b/solution.py
@@ -15,10 +15,10 @@
 def fused_kernel(
     groups, ranks, x_ref, old_ref, keep_ref, owner_ref, og_ref,
     proj_ref, gin_ref, wg_ref,
-    comp, pack, unpacked, xhat, normed, stripes, acc, dn_send, dn_recv, dot_send, dot_recv,
+    comp, pack, unpacked, xhat, normed, stripes, acc, dn_send, dn_recv, relay, dot_send, dot_recv,
     sib_send, sib_recv, up_send, up_recv, down_send, down_recv,
     pack_ss, pack_rs, sib_ss, sib_rs, up_ss, up_rs, down_ss, down_rs,
-    gup_ss, gdown_ss, gsib_ss, gather_rs, dn_ss, dn_rs, dot_ss, dot_rs,
+    gup_ss, gdown_ss, gsib_ss, gather_rs, dn_ss, dn_rs, relay_rs, dot_ss, dot_rs,
 ):
     dp = lax.axis_index("dp")
     ten = lax.axis_index("tensor")
@@ -130,12 +130,12 @@
 
     @pl.when(z == 0)
     def _():
-        for c in range(chips - 1, 0, -1):
+        for c in range(chips - 1, 1, -1):
             up_first(c)
 
     @pl.when(z == chips - 1)
     def _():
-        for c in range(chips - 1):
+        for c in range(chips - 2):
             down_first(c)
 
     def chain(k):
@@ -180,12 +180,34 @@
     def gather_sib(d):
         return remote(stripes.at[d], stripes.at[d], gsib_ss.at[d], gather_rs.at[d], dp=sibling)
 
-    def dn_copy(d):
-        k = lax.rem(d // per - ten + groups, groups)
+    half = rows // 2
+
+    def flip(bit):
+        x, y = ten % 2, ten // 2
+        return y * 2 + (1 - x) if bit == 1 else (1 - y) * 2 + x
+
+    def rows_of(h):
+        return pl.ds(h * half, half)
+
+    def dn_copy(d, bit, h):
         j = d % per
         return remote(
-            dn_send.at[d], dn_recv.at[k, j], dn_ss.at[d], dn_rs.at[k, j], tensor=d // per
+            dn_send.at[d, rows_of(h)], dn_recv.at[bit - 1, j, rows_of(h)],
+            dn_ss.at[d, h], dn_rs.at[bit - 1, j, h], tensor=flip(bit),
         )
+
+    def relay_copy(d, bit):
+        h = bit - 1
+        return remote(
+            dn_send.at[d, rows_of(h)], relay.at[d], dn_ss.at[d, h], relay_rs.at[d],
+            tensor=flip(bit),
+        )
+
+    def is_near(d, bit):
+        return d // per == flip(bit)
+
+    def is_far(d):
+        return (d // per != ten) & (d // per != flip(1)) & (d // per != flip(2))
 
     def use(d):
         part = lax.dot_general(
@@ -193,9 +215,15 @@
         ).astype(BF16)
         dn_send[d] = part
 
-        @pl.when(d // per != ten)
-        def _():
-            dn_copy(d).start()
+        @pl.when(is_far(d))
+        def _():
+            relay_copy(d, 1).start()
+            relay_copy(d, 2).start()
+
+        for bit in (1, 2):
+            @pl.when(is_near(d, bit))
+            def _():
+                dn_copy(d, bit, bit - 1).start()
 
         dot_send[...] += jnp.sum(
             (part.astype(F32) * strip(xhat, d)).reshape(rows // 8, 8, tokens), axis=0
@@ -204,6 +232,28 @@
             strip(normed, d), stripes[d], (((0,), (0,)), ((), ())), preferred_element_type=F32
         )
 
+    def pass_on(d):
+        for bit in (1, 2):
+            @pl.when(is_near(d, bit))
+            def _():
+                h = 2 - bit
+                relay_copy(d, 3 - bit).wait_recv()
+                mine = dn_send[d, rows_of(h)].astype(F32)
+                dn_send[d, rows_of(h)] = (mine + relay[d].astype(F32)).astype(BF16)
+                dn_copy(d, bit, h).start()
+
+    def pass_on_pair(s):
+        @pl.when(z - s >= 0)
+        def _():
+            pass_on(dp - 2 * s)
+            pass_on((z - s) * 2 + 1 - core)
+
+        if s > 0:
+            @pl.when(z + s < chips)
+            def _():
+                pass_on(dp + 2 * s)
+                pass_on((z + s) * 2 + 1 - core)
+
     acc[...] = jnp.zeros_like(acc)
     dot_send[...] = jnp.zeros_like(dot_send)
 
@@ -223,6 +273,7 @@
         gather_sib(d).wait_recv()
         use(d)
 
+    from_sibling(z)
     for s in range(1, chips):
         chain(s - 1)
 
@@ -249,7 +300,15 @@
             gather_sib(d).start()
 
         if s == 1:
-            from_sibling(z)
+            @pl.when(z == 0)
+            def _():
+                up_first(1)
+
+            @pl.when(z == chips - 1)
+            def _():
+                down_first(chips - 2)
+
+        pass_on_pair(s - 1)
 
         @pl.when(z - s >= 0)
         def _():
@@ -266,6 +325,7 @@
 
     for k in range(1, groups):
         dot_copy(k).start()
+    pass_on_pair(chips - 1)
     proj_ref[...] = acc[...].astype(BF16)
 
     sib_total = grad_part(dp)
@@ -290,11 +350,10 @@
     for j in range(per):
         at = ten * per + j
         full = dn_send[at].astype(F32)
-        for k in range(1, groups):
-            remote(
-                dn_send.at[at], dn_recv.at[k, j], dn_ss.at[at], dn_rs.at[k, j], tensor=peer(k)
-            ).wait_recv()
-            full = full + dn_recv[k, j].astype(F32)
+        for bit in (1, 2):
+            for h in (0, 1):
+                dn_copy(at, bit, h).wait_recv()
+            full = full + dn_recv[bit - 1, j].astype(F32)
         acc_t = inv * (full - strip(xhat, at) * mean)
         xhat[pl.ds(pl.multiple_of(at * rows, 16), rows), :] = acc_t
     for j in range(share // 128):
@@ -329,7 +388,8 @@
     for d in range(ranks):
         @pl.when(d // per != ten)
         def _():
-            dn_copy(d).wait_send()
+            for h in (0, 1):
+                dn_copy(d, 1, h).wait_send()
 
 
 def fused(groups, ranks, inputs, old_weight, keep_cols, owner, out_grad):
@@ -361,18 +421,19 @@
             pltpu.VMEM((ranks,) + stripe, BF16),
             pltpu.VMEM((tokens, cols), F32),
             pltpu.VMEM((ranks, rows, tokens), BF16),
-            pltpu.VMEM((groups, per, rows, tokens), BF16),
+            pltpu.VMEM((2, per, rows, tokens), BF16),
+            pltpu.VMEM((ranks, rows // 2, tokens), BF16),
             pltpu.VMEM((8, tokens), F32),
             pltpu.VMEM((groups, 8, tokens), F32),
         ]
         + [pltpu.VMEM((chips,) + stripe, BF16)] * 6
         + [dma((groups,))] * 2
         + [dma((chips,))] * 6
-        + [dma((ranks,))] * 5
-        + [dma((groups, per))]
+        + [dma((ranks,))] * 4
+        + [dma((ranks, 2)), dma((2, per, 2)), dma((ranks,))]
         + [dma((groups,))] * 2,
         compiler_params=pltpu.CompilerParams(
-            collective_id=0, has_side_effects=True, vmem_limit_bytes=56 * 1024 * 1024
+            collective_id=0, has_side_effects=True, vmem_limit_bytes=26 * 1024 * 1024
         ),
     )(inputs, old_weight, keep_cols.reshape(-1, 128), owner, out_grad)
 
@@ -433,7 +494,7 @@
 
     def local(inputs, old_weight, keep_cols, owner, out_grad):
         rows, share = old_weight.shape[0], inputs.shape[1] // groups
-        fits = rows % 16 == 0 and share % 128 == 0 and ranks % groups == 0 and ranks % 2 == 0
+        fits = rows % 32 == 0 and share % 128 == 0 and groups == 4 and ranks % 4 == 0
         if fits:
             return fused(groups, ranks, inputs, old_weight, keep_cols, owner, out_grad)
         return plain(inputs, old_weight, keep_cols, owner, out_grad)

time: 68 us -> 66.7 us (0.981)
  Pallas kernels: 62.8 us -> 59.1 us
  local copies, waits for them, and re-layouts: 4.18 us -> 6.74 us
    pallas_call x1, Pallas kernels: 62.8 us -> 59.1 us  [fused(): pl.pallas_call(functools.partial(fused_kernel, groups, ranks), out_shape=...]
    unnamed x5 -> x13, local copies, waits for them, and re-layouts: 4.18 us -> 6.74 us
where the time goes in v2:
time: 66.7 us; the launch traced here: 66.4 us
  Pallas kernels  59.1 us (89%)
  local copies, waits for them, and re-layouts  6.74 us (10%)
    pallas_call x1, Pallas kernels, fused(): pl.pallas_call(functools.partial(fused_kernel, groups, ranks), out_shape=...  59.1 us
    unnamed x13, local copies, waits for them, and re-layouts  6.74 us

profile of v2, /device:TPU:6, one launch (start us, length us, event | category | flops | bytes accessed | tf_op | source)
XLA Modules:
  0.0 66.4 jit_solution(8818623868506026521)
XLA Ops:
  0.6 0.0 copy-start
  0.6 1.3 %copy-done = bf16[256,2560]{1,0:T(8,128)(2,1)S(1)} copy-done((bf16[256,2560]{1,0:T(8,128)(2,1)S(1)}, bf16[256,2560]{1,0:T(8,128)(2,1)}, u32[]{:S(2)}) %copy-start) | copy-done | bytes 1310744
  1.9 0.0 copy-start.1
  2.0 1.0 %copy-done.1 = bf16[320,512]{1,0:T(8,128)(2,1)S(1)} copy-done((bf16[320,512]{1,0:T(8,128)(2,1)S(1)}, bf16[320,512]{1,0:T(8,128)(2,1)}, u32[]{:S(2)}) %copy-start.1) | copy-done | bytes 327704
  2.9 0.0 copy-start.2
  2.9 0.9 %copy-done.2 = bf16[256,384]{1,0:T(8,128)(2,1)S(1)} copy-done((bf16[256,384]{1,0:T(8,128)(2,1)S(1)}, bf16[256,384]{1,0:T(8,128)(2,1)}, u32[]{:S(2)}) %copy-start.2) | copy-done | bytes 196632
  3.8 0.0 copy-start.3
  3.9 0.7 %copy-done.3 = s32[1536]{0:T(1024)S(1)} copy-done((s32[1536]{0:T(1024)S(1)}, s32[1536]{0:T(1024)}, u32[]{:S(2)}) %copy-start.3) | copy-done | bytes 6168
  4.5 0.0 copy-start.4
  4.5 0.7 copy-done.4
  5.2 59.1 %shard_map.76 = (bf16[256,384]{1,0:T(8,128)(2,1)S(1)}, bf16[256,640]{1,0:T(8,128)(2,1)S(1)}, f32[320,384]{1,0:T(8,128)S(1)}) custom-call(bf16[256,2560]{1,0:T(8,128)(2,1)S(1)} %copy-done, bf16[320,512]{1,0:T(8,128)(2,1)S(1)} %copy-done.1, s32[12,128]{1,0:T(8,128)S(1)} %bitcast.1, s32[12]{0:T(128)S(1)} %copy-done.4, bf16[256,384]{1,0:T(8,128)(2,1)S(1)} %copy-done.2), custom_call_target="tpu_custom_call" | custom-call | tf_op jit(solution)/shard_map/pallas_call | solution.py:406
  64.3 0.7 %copy.11 = bf16[256,384]{1,0:T(8,128)(2,1)} copy(bf16[256,384]{1,0:T(8,128)(2,1)S(1)} %get-tuple-element.6) | data formatting | bytes 393216
  64.9 0.7 %copy.12 = bf16[256,640]{1,0:T(8,128)(2,1)} copy(bf16[256,640]{1,0:T(8,128)(2,1)S(1)} %get-tuple-element.7) | data formatting | bytes 655360
  65.7 0.8 %copy.13 = f32[320,384]{1,0:T(8,128)} copy(f32[320,384]{1,0:T(8,128)S(1)} %get-tuple-element.8) | data formatting | bytes 983040
Async XLA Ops:
  0.6 1.3 %copy-start = (bf16[256,2560]{1,0:T(8,128)(2,1)S(1)}, bf16[256,2560]{1,0:T(8,128)(2,1)}, u32[]{:S(2)}) copy-start(bf16[256,2560]{1,0:T(8,128)(2,1)} %x_ref.1) | copy-start | bytes 3932164
  1.9 1.0 %copy-start.1 = (bf16[320,512]{1,0:T(8,128)(2,1)S(1)}, bf16[320,512]{1,0:T(8,128)(2,1)}, u32[]{:S(2)}) copy-start(bf16[320,512]{1,0:T(8,128)(2,1)} %old_ref.1) | copy-start | bytes 983044
  2.9 0.9 %copy-start.2 = (bf16[256,384]{1,0:T(8,128)(2,1)S(1)}, bf16[256,384]{1,0:T(8,128)(2,1)}, u32[]{:S(2)}) copy-start(bf16[256,384]{1,0:T(8,128)(2,1)} %og_ref.1) | copy-start | bytes 589828
  3.8 0.7 %copy-start.3 = (s32[1536]{0:T(1024)S(1)}, s32[1536]{0:T(1024)}, u32[]{:S(2)}) copy-start(s32[1536]{0:T(1024)} %param.7) | copy-start | bytes 18436
  4.5 0.7 copy-start.4

commit v3 on v2

--- a/solution.py
+++ b/solution.py
@@ -132,28 +132,46 @@
     def _():
         for c in range(chips - 1, 1, -1):
             up_first(c)
+            if c > 2:
+                up_copy(c).wait_send()
 
     @pl.when(z == chips - 1)
     def _():
         for c in range(chips - 2):
             down_first(c)
+            if c < chips - 3:
+                down_copy(c).wait_send()
+
+    def chain_up(up):
+        mine = pair_sum(up)
+        up_copy(up).wait_recv()
+        up_send[up] = (mine + up_recv[up].astype(F32)).astype(BF16)
+        up_copy(up).start()
+
+    def chain_down(down):
+        mine = pair_sum(down)
+        down_copy(down).wait_recv()
+        down_send[down] = (mine + down_recv[down].astype(F32)).astype(BF16)
+        down_copy(down).start()
+
+    @pl.when((z == 1) & (z < chips - 1))
+    def _():
+        chain_up(chips - 1)
+
+    @pl.when((z == chips - 2) & (z > 0))
+    def _():
+        chain_down(0)
 
     def chain(k):
         up, down = chips - 1 - k, k
 
-        @pl.when((z > 0) & (z < up))
-        def _():
-            mine = pair_sum(up)
-            up_copy(up).wait_recv()
-            up_send[up] = (mine + up_recv[up].astype(F32)).astype(BF16)
-            up_copy(up).start()
-
-        @pl.when((z < chips - 1) & (z > down))
-        def _():
-            mine = pair_sum(down)
-            down_copy(down).wait_recv()
-            down_send[down] = (mine + down_recv[down].astype(F32)).astype(BF16)
-            down_copy(down).start()
+        @pl.when((z > (1 if k == 0 else 0)) & (z < up))
+        def _():
+            chain_up(up)
+
+        @pl.when((z < chips - (2 if k == 0 else 1)) & (z > down))
+        def _():
+            chain_down(down)
 
     places = [jnp.int32(0) for _ in range(own)]
     count = jnp.int32(0)
@@ -275,8 +293,6 @@
 
     from_sibling(z)
     for s in range(1, chips):
-        chain(s - 1)
-
         @pl.when(z - s >= 0)
         def _():
             d = dp - 2 * s
@@ -309,6 +325,10 @@
                 down_first(chips - 2)
 
         pass_on_pair(s - 1)
+
+        if s == max(chips - 2, 1):
+            for k in range(chips - 1):
+                chain(k)
 
         @pl.when(z - s >= 0)
         def _():
@@ -366,11 +386,11 @@
     for c in range(chips):
         sib_copy(c).wait_send()
 
-        @pl.when(c > z)
+        @pl.when((c > z) & ((z > 0) | (c <= 2)))
         def _():
             up_copy(c).wait_send()
 
-        @pl.when(c < z)
+        @pl.when((c < z) & ((z < chips - 1) | (c >= chips - 3)))
         def _():
             down_copy(c).wait_send()
 

time: 66.7 us -> 59.5 us (0.89)
  Pallas kernels: 59.1 us -> 51.8 us
    pallas_call x1, Pallas kernels: 59.1 us -> 51.8 us  [fused(): pl.pallas_call(functools.partial(fused_kernel, groups, ranks), out_shape=...]
where the time goes in v3:
time: 59.5 us; the launch traced here: 59.2 us
  Pallas kernels  51.8 us (87%)
  local copies, waits for them, and re-layouts  6.74 us (11%)
  between operations  0.65 us (1%)
    pallas_call x1, Pallas kernels, fused(): pl.pallas_call(functools.partial(fused_kernel, groups, ranks), out_shape=...  51.8 us
    unnamed x13, local copies, waits for them, and re-layouts  6.74 us

profile of v3, /device:TPU:6, one launch (start us, length us, event | category | flops | bytes accessed | tf_op | source)
XLA Modules:
  0.0 59.2 jit_solution(608141109813747153)
XLA Ops:
  0.6 0.0 copy-start
  0.6 1.3 %copy-done = bf16[256,2560]{1,0:T(8,128)(2,1)S(1)} copy-done((bf16[256,2560]{1,0:T(8,128)(2,1)S(1)}, bf16[256,2560]{1,0:T(8,128)(2,1)}, u32[]{:S(2)}) %copy-start) | copy-done | bytes 1310744
  1.9 0.0 copy-start.1
  2.0 1.0 %copy-done.1 = bf16[320,512]{1,0:T(8,128)(2,1)S(1)} copy-done((bf16[320,512]{1,0:T(8,128)(2,1)S(1)}, bf16[320,512]{1,0:T(8,128)(2,1)}, u32[]{:S(2)}) %copy-start.1) | copy-done | bytes 327704
  2.9 0.0 copy-start.2
  2.9 0.9 %copy-done.2 = bf16[256,384]{1,0:T(8,128)(2,1)S(1)} copy-done((bf16[256,384]{1,0:T(8,128)(2,1)S(1)}, bf16[256,384]{1,0:T(8,128)(2,1)}, u32[]{:S(2)}) %copy-start.2) | copy-done | bytes 196632
  3.8 0.0 copy-start.3
  3.9 0.7 %copy-done.3 = s32[1536]{0:T(1024)S(1)} copy-done((s32[1536]{0:T(1024)S(1)}, s32[1536]{0:T(1024)}, u32[]{:S(2)}) %copy-start.3) | copy-done | bytes 6168
  4.5 0.0 copy-start.4
  4.5 0.7 %copy-done.4 = s32[12]{0:T(128)S(1)} copy-done((s32[12]{0:T(128)S(1)}, s32[12]{0:T(128)}, u32[]{:S(2)}) %copy-start.4) | copy-done | bytes 72
  5.2 51.8 %shard_map.76 = (bf16[256,384]{1,0:T(8,128)(2,1)S(1)}, bf16[256,640]{1,0:T(8,128)(2,1)S(1)}, f32[320,384]{1,0:T(8,128)S(1)}) custom-call(bf16[256,2560]{1,0:T(8,128)(2,1)S(1)} %copy-done, bf16[320,512]{1,0:T(8,128)(2,1)S(1)} %copy-done.1, s32[12,128]{1,0:T(8,128)S(1)} %bitcast.1, s32[12]{0:T(128)S(1)} %copy-done.4, bf16[256,384]{1,0:T(8,128)(2,1)S(1)} %copy-done.2), custom_call_target="tpu_custom_call" | custom-call | tf_op jit(solution)/shard_map/pallas_call | solution.py:426
  57.0 0.7 %copy.11 = bf16[256,384]{1,0:T(8,128)(2,1)} copy(bf16[256,384]{1,0:T(8,128)(2,1)S(1)} %get-tuple-element.6) | data formatting | bytes 393216
  57.7 0.7 %copy.12 = bf16[256,640]{1,0:T(8,128)(2,1)} copy(bf16[256,640]{1,0:T(8,128)(2,1)S(1)} %get-tuple-element.7) | data formatting | bytes 655360
  58.4 0.8 %copy.13 = f32[320,384]{1,0:T(8,128)} copy(f32[320,384]{1,0:T(8,128)S(1)} %get-tuple-element.8) | data formatting | bytes 983040
Async XLA Ops:
  0.6 1.3 %copy-start = (bf16[256,2560]{1,0:T(8,128)(2,1)S(1)}, bf16[256,2560]{1,0:T(8,128)(2,1)}, u32[]{:S(2)}) copy-start(bf16[256,2560]{1,0:T(8,128)(2,1)} %x_ref.1) | copy-start | bytes 3932164
  1.9 1.0 %copy-start.1 = (bf16[320,512]{1,0:T(8,128)(2,1)S(1)}, bf16[320,512]{1,0:T(8,128)(2,1)}, u32[]{:S(2)}) copy-start(bf16[320,512]{1,0:T(8,128)(2,1)} %old_ref.1) | copy-start | bytes 983044
  2.9 0.9 %copy-start.2 = (bf16[256,384]{1,0:T(8,128)(2,1)S(1)}, bf16[256,384]{1,0:T(8,128)(2,1)}, u32[]{:S(2)}) copy-start(bf16[256,384]{1,0:T(8,128)(2,1)} %og_ref.1) | copy-start | bytes 589828
  3.8 0.7 %copy-start.3 = (s32[1536]{0:T(1024)S(1)}, s32[1536]{0:T(1024)}, u32[]{:S(2)}) copy-start(s32[1536]{0:T(1024)} %param.7) | copy-start | bytes 18436
  4.5 0.7 %copy-start.4 = (s32[12]{0:T(128)S(1)}, s32[12]{0:T(128)}, u32[]{:S(2)}) copy-start(s32[12]{0:T(128)} %owner_ref.1) | copy-start | bytes 148

commit v4 on v3

--- a/solution.py
+++ b/solution.py
@@ -326,7 +326,7 @@
 
         pass_on_pair(s - 1)
 
-        if s == max(chips - 2, 1):
+        if s == chips - 1:
             for k in range(chips - 1):
                 chain(k)
 

time: 59.5 us -> 58.6 us (0.985)
  Pallas kernels: 51.8 us -> 50.9 us
    pallas_call x1, Pallas kernels: 51.8 us -> 50.9 us  [fused(): pl.pallas_call(functools.partial(fused_kernel, groups, ranks), out_shape=...]
where the time goes in v4:
time: 58.6 us; the launch traced here: 58.3 us
  Pallas kernels  50.9 us (87%)
  local copies, waits for them, and re-layouts  6.74 us (12%)
  between operations  0.65 us (1%)
    pallas_call x1, Pallas kernels, fused(): pl.pallas_call(functools.partial(fused_kernel, groups, ranks), out_shape=...  50.9 us
    unnamed x13, local copies, waits for them, and re-layouts  6.74 us

profile of v4, /device:TPU:6, one launch (start us, length us, event | category | flops | bytes accessed | tf_op | source)
XLA Modules:
  0.0 58.3 jit_solution(12839148129921590198)
XLA Ops:
  0.6 0.0 copy-start
  0.6 1.3 %copy-done = bf16[256,2560]{1,0:T(8,128)(2,1)S(1)} copy-done((bf16[256,2560]{1,0:T(8,128)(2,1)S(1)}, bf16[256,2560]{1,0:T(8,128)(2,1)}, u32[]{:S(2)}) %copy-start) | copy-done | bytes 1310744
  1.9 0.0 copy-start.1
  2.0 1.0 %copy-done.1 = bf16[320,512]{1,0:T(8,128)(2,1)S(1)} copy-done((bf16[320,512]{1,0:T(8,128)(2,1)S(1)}, bf16[320,512]{1,0:T(8,128)(2,1)}, u32[]{:S(2)}) %copy-start.1) | copy-done | bytes 327704
  2.9 0.0 copy-start.2
  2.9 0.9 %copy-done.2 = bf16[256,384]{1,0:T(8,128)(2,1)S(1)} copy-done((bf16[256,384]{1,0:T(8,128)(2,1)S(1)}, bf16[256,384]{1,0:T(8,128)(2,1)}, u32[]{:S(2)}) %copy-start.2) | copy-done | bytes 196632
  3.8 0.0 copy-start.3
  3.9 0.7 %copy-done.3 = s32[1536]{0:T(1024)S(1)} copy-done((s32[1536]{0:T(1024)S(1)}, s32[1536]{0:T(1024)}, u32[]{:S(2)}) %copy-start.3) | copy-done | bytes 6168
  4.5 0.0 copy-start.4
  4.5 0.7 %copy-done.4 = s32[12]{0:T(128)S(1)} copy-done((s32[12]{0:T(128)S(1)}, s32[12]{0:T(128)}, u32[]{:S(2)}) %copy-start.4) | copy-done | bytes 72
  5.2 50.9 %shard_map.76 = (bf16[256,384]{1,0:T(8,128)(2,1)S(1)}, bf16[256,640]{1,0:T(8,128)(2,1)S(1)}, f32[320,384]{1,0:T(8,128)S(1)}) custom-call(bf16[256,2560]{1,0:T(8,128)(2,1)S(1)} %copy-done, bf16[320,512]{1,0:T(8,128)(2,1)S(1)} %copy-done.1, s32[12,128]{1,0:T(8,128)S(1)} %bitcast.1, s32[12]{0:T(128)S(1)} %copy-done.4, bf16[256,384]{1,0:T(8,128)(2,1)S(1)} %copy-done.2), custom_call_target="tpu_custom_call" | custom-call | tf_op jit(solution)/shard_map/pallas_call | solution.py:426
  56.1 0.7 %copy.11 = bf16[256,384]{1,0:T(8,128)(2,1)} copy(bf16[256,384]{1,0:T(8,128)(2,1)S(1)} %get-tuple-element.6) | data formatting | bytes 393216
  56.8 0.7 %copy.12 = bf16[256,640]{1,0:T(8,128)(2,1)} copy(bf16[256,640]{1,0:T(8,128)(2,1)S(1)} %get-tuple-element.7) | data formatting | bytes 655360
  57.5 0.8 %copy.13 = f32[320,384]{1,0:T(8,128)} copy(f32[320,384]{1,0:T(8,128)S(1)} %get-tuple-element.8) | data formatting | bytes 983040
Async XLA Ops:
  0.6 1.3 %copy-start = (bf16[256,2560]{1,0:T(8,128)(2,1)S(1)}, bf16[256,2560]{1,0:T(8,128)(2,1)}, u32[]{:S(2)}) copy-start(bf16[256,2560]{1,0:T(8,128)(2,1)} %x_ref.1) | copy-start | bytes 3932164
  1.9 1.0 %copy-start.1 = (bf16[320,512]{1,0:T(8,128)(2,1)S(1)}, bf16[320,512]{1,0:T(8,128)(2,1)}, u32[]{:S(2)}) copy-start(bf16[320,512]{1,0:T(8,128)(2,1)} %old_ref.1) | copy-start | bytes 983044
  2.9 0.9 %copy-start.2 = (bf16[256,384]{1,0:T(8,128)(2,1)S(1)}, bf16[256,384]{1,0:T(8,128)(2,1)}, u32[]{:S(2)}) copy-start(bf16[256,384]{1,0:T(8,128)(2,1)} %og_ref.1) | copy-start | bytes 589828
  3.8 0.7 %copy-start.3 = (s32[1536]{0:T(1024)S(1)}, s32[1536]{0:T(1024)}, u32[]{:S(2)}) copy-start(s32[1536]{0:T(1024)} %param.7) | copy-start | bytes 18436
  4.5 0.7 %copy-start.4 = (s32[12]{0:T(128)S(1)}, s32[12]{0:T(128)}, u32[]{:S(2)}) copy-start(s32[12]{0:T(128)} %owner_ref.1) | copy-start | bytes 148
